TPU v7x, 1024 devices: a whole 4x8x16 slice. The times are simulated.
1024 devices in a mesh: sy: 16 (over y, core), sz: 16 (over z), traj: 4 (over x).
Axes of the slice: x: 4, y: 8, z: 16, core: 2. Of those that a mesh axis runs over, the one named last changes fastest.
Arguments:
- coeffs: float32 [512, 256], P('traj'), may hold values from -6 to 6
- basis: bfloat16 [256, 64, 64, 128], P(None, 'sy', 'sz'), may hold values from -0.375 to 0.375
- damping: float32 [256], replicated, may hold values from 0.2 to 2
- w_in: float32 [8, 7], replicated, may hold values from -3 to 3
- b_in: float32 [8], replicated, may hold values from -3 to 3
- w_out: float32 [8], replicated, may hold values from -2 to 2
Outputs:
- tendency: float32 [512, 256], P('traj')
All inputs are finite; a program needn't handle non-finite values.
Results may differ from a plain program's by a relative error of at most 0.0072.
Values may be sent and summed in bfloat16 or wider, within the bound.
A program may use at most 32 MiB of HBM per device.

v0:
```python
import jax
import jax.numpy as jnp
from jax import lax
from jax.sharding import PartitionSpec as P


def padded_2(block, sides, width):
    for axis, dim in sides:
        count = lax.axis_size(axis)
        forward = [(i, i + 1) for i in range(count - 1)]
        backward = [(target, source) for source, target in forward]
        low = lax.ppermute(
            lax.slice_in_dim(block, block.shape[dim] - width, None, axis=dim), axis, forward
        )
        high = lax.ppermute(lax.slice_in_dim(block, 0, width, axis=dim), axis, backward)
        block = jnp.concatenate([low, block, high], axis=dim)
    return block


def closure_of(padded, w_in, b_in, w_out):
    center = padded[:, 1:-1, 1:-1, 1:-1]
    taps = (
        center,
        padded[:, :-2, 1:-1, 1:-1],
        padded[:, 2:, 1:-1, 1:-1],
        padded[:, 1:-1, 1:-1, :-2],
        padded[:, 1:-1, 1:-1, 2:],
        padded[:, 1:-1, :-2, 1:-1],
        padded[:, 1:-1, 2:, 1:-1],
    )
    total = jnp.zeros(center.shape, jnp.float32)
    for hidden in range(w_in.shape[0]):
        inner = b_in[hidden] + w_in[hidden, 0] * taps[0]
        for index in range(1, 7):
            inner = inner + w_in[hidden, index] * taps[index]
        total = total + w_out[hidden] * jnp.tanh(inner)
    return total


def local(coeffs, basis, damping, w_in, b_in, w_out):
    batch = coeffs.shape[0]
    modes, rows, depth, width = basis.shape
    flat = basis.reshape(modes, rows * depth * width)
    cells_all = rows * depth * width * lax.axis_size("sy") * lax.axis_size("sz")
    scale = (modes / cells_all) ** 0.5

    def rate(state):
        state_b = state.astype(jnp.bfloat16)
        field = jnp.dot(state_b, flat, preferred_element_type=jnp.float32).reshape(
            batch, rows, depth, width
        )
        padded = padded_2(field, (("sy", 1), ("sz", 2)), 1)
        padded = jnp.pad(padded, ((0, 0), (0, 0), (0, 0), (1, 1)))
        closure = closure_of(padded, w_in, b_in, w_out).astype(jnp.bfloat16)
        partial_sum = lax.dot_general(
            closure.reshape(batch, rows * depth * width),
            flat,
            (((1,), (1,)), ((), ())),
            preferred_element_type=jnp.float32,
        )
        modal = lax.psum(partial_sum, ("sy", "sz"))
        return -damping * state + scale * modal

    first = rate(coeffs)
    second = rate(coeffs + 0.5 * first)
    return 0.5 * (first + second)


def solution(mesh):
    return jax.shard_map(
        local,
        mesh=mesh,
        in_specs=(P("traj", None), P(None, "sy", "sz", None), P(), P(), P(), P()),
        out_specs=P("traj", None),
        check_vma=False,
    )
```

profile of v0, /device:TPU:1, one launch (start us, length us, event | category | flops | bytes accessed | tf_op | source)
XLA Modules:
  0.0 827.7 jit_solution(14259460143457208074)
XLA Ops:
  6.5 0.0 all-reduce.5.cloned.1.call-start
  6.5 1.9 reshape.10
  8.4 0.0 copy-start.4
  8.4 0.5 copy.7
  9.0 0.0 copy-done
  9.0 0.0 copy-start.5
  9.0 0.0 copy-start.3
  9.0 0.4 fusion.27
  9.5 4.6 collective-permute-start
  14.1 12.8 %collective-permute-start.1 = (f32[128,1,4,128]{0,3,2,1:T(8,128)S(1)}, f32[128,1,4,128]{0,3,2,1:T(8,128)S(1)}, u32[]{:S(2)}, u32[]{:S(2)}) collective-permute-start(f32[128,1,4,128]{0,3,2,1:T(8,128)S(1)} %get-tuple-element.12), channel_id=1, source_target_pairs={{64,0},{128,64},{192,128},{256,192},{320,256},{384,320},{448,384},... | collective-permute-start | bytes 786440 | tf_op jit(solution)/shard_map/ppermute | solution.py:15
  26.8 0.0 copy-done.4
  26.9 0.7 fusion.42
  27.5 0.0 collective-permute-done
  27.5 0.5 collective-permute-done.1
  28.0 0.1 pad_maximum_fusion.21
  28.0 1.3 collective-permute-start.2
  29.4 1.3 collective-permute-start.3
  30.7 0.0 copy-done.5
  30.7 0.7 fusion.43
  31.4 0.0 copy-done.3
  31.4 0.7 fusion.41
  32.1 0.7 fusion.40
  32.8 0.7 fusion.39
  33.5 4.3 collective-permute-done.2
  37.8 3.8 collective-permute-done.3
  41.6 0.3 select_maximum_fusion.4
  41.9 0.0 copy-done.1
  41.9 0.0 copy-start.6
  41.9 50.6 %convolution_bitcast_fusion.1 = f32[128,256]{1,0:T(8,128)} fusion(bf16[256,4,4,128]{3,2,1,0:T(4,128)(2,1)S(1)} %copy-done.1, f32[128,4,4,128]{0,3,2,1:T(8,128)S(1)} %fusion.27, f32[128,1,4,128]{0,3,2,1:T(8,128)S(1)} %collective-permute-done.1, f32[128,1,4,128]{0,3,2,1:T(8,128)S(1)} %collective-permute-done, ...), kind=kOutput, calls=%fused_computation.12 | convolution fusion | flops 169869312 | bytes 5636384 | tf_op jit(solution)/shard_map/dot_general | solution.py:55
  92.5 0.0 all-reduce.5.cloned.1.call-update
  92.5 0.0 all-reduce.7.cloned.1.call-start
  92.6 330.9 %all-reduce.5.cloned.1.call-done = f32[128,256]{1,0:T(8,128)} async-done(((f32[128,256]{1,0:T(8,128)}), f32[128,256]{1,0:T(8,128)}) %all-reduce.5.cloned.1.call-update) | async-done | bytes 131088 | tf_op jit(solution)/shard_map/psum | solution.py:61
  423.4 1.3 fusion.25
  424.8 2.1 collective-permute-start.4
  427.0 2.2 collective-permute-start.5
  429.2 1.1 collective-permute-done.4
  430.3 4.4 collective-permute-done.5
  434.7 0.1 pad_maximum_fusion.18
  434.7 2.7 collective-permute-start.6
  437.4 1.5 collective-permute-start.7
  438.9 3.6 collective-permute-done.6
  442.5 4.1 collective-permute-done.7
  446.6 0.3 select_maximum_fusion
  446.9 50.6 %convolution_bitcast_fusion = f32[128,256]{1,0:T(8,128)} fusion(bf16[256,4,4,128]{3,2,1,0:T(4,128)(2,1)S(1)} %copy-done.1, f32[128,4,4,128]{0,3,2,1:T(8,128)S(1)} %fusion.25, f32[128,1,4,128]{0,3,2,1:T(8,128)S(1)} %collective-permute-done.5, f32[128,1,4,128]{0,3,2,1:T(8,128)S(1)} %collective-permute-done.4, ...), kind=kOutput, calls=%fused_computation.11 | convolution fusion | flops 169869312 | bytes 5636384 | tf_op jit(solution)/shard_map/dot_general | solution.py:55
  497.5 0.0 all-reduce.7.cloned.1.call-update
  497.6 321.7 %all-reduce.7.cloned.1.call-done = f32[128,256]{1,0:T(8,128)} async-done(((f32[128,256]{1,0:T(8,128)}), f32[128,256]{1,0:T(8,128)}) %all-reduce.7.cloned.1.call-update) | async-done | bytes 131088 | tf_op jit(solution)/shard_map/psum | solution.py:61
  819.3 0.0 copy-done.2
  819.3 1.6 add_multiply_fusion
  (7 shorter events, 0.1 us)
Async XLA Ops:
  6.5 2.4 copy-start
  6.5 416.9 %all-reduce.5.cloned.1.call-start = ((), (), s32[]{:S(2)}) async-start(), calls=%async_computation | async-start | bytes 262144 | tf_op jit(solution)/shard_map/psum | solution.py:61
  8.4 18.4 %copy-start.4 = (f32[8]{0:T(128)S(1)}, f32[8]{0:T(128)}, u32[]{:S(2)}) copy-start(f32[8]{0:T(128)} %param.11) | copy-start | bytes 100
  9.0 21.7 %copy-start.5 = (f32[8]{0:T(128)S(1)}, f32[8]{0:T(128)}, u32[]{:S(2)}) copy-start(f32[8]{0:T(128)} %param.10) | copy-start | bytes 100
  9.0 22.4 %copy-start.3 = (f32[8,7]{1,0:T(8,128)S(1)}, f32[8,7]{1,0:T(8,128)}, u32[]{:S(2)}) copy-start(f32[8,7]{1,0:T(8,128)} %param.9) | copy-start | bytes 676
  9.5 18.1 %collective-permute-start = (f32[128,1,4,128]{0,3,2,1:T(8,128)S(1)}, f32[128,1,4,128]{0,3,2,1:T(8,128)S(1)}, u32[]{:S(2)}, u32[]{:S(2)}) collective-permute-start(f32[128,1,4,128]{0,3,2,1:T(8,128)S(1)} %get-tuple-element.11), channel_id=1, source_target_pairs={{0,64},{64,128},{128,192},{192,256},{256,320},{320,384},{384,448},... | collective-permute-start | bytes 786440 | tf_op jit(solution)/shard_map/ppermute | solution.py:12
  14.1 13.9 %collective-permute-start.1 = (f32[128,1,4,128]{0,3,2,1:T(8,128)S(1)}, f32[128,1,4,128]{0,3,2,1:T(8,128)S(1)}, u32[]{:S(2)}, u32[]{:S(2)}) collective-permute-start(f32[128,1,4,128]{0,3,2,1:T(8,128)S(1)} %get-tuple-element.12), channel_id=1, source_target_pairs={{64,0},{128,64},{192,128},{256,192},{320,256},{384,320},{448,384},... | collective-permute-start | bytes 786440 | tf_op jit(solution)/shard_map/ppermute | solution.py:15
  28.0 9.7 %collective-permute-start.2 = (f32[128,6,1,128]{0,3,2,1:T(8,128)S(1)}, f32[128,6,1,128]{0,3,2,1:T(8,128)S(1)}, u32[]{:S(2)}, u32[]{:S(2)}) collective-permute-start(f32[128,6,1,128]{0,3,2,1:T(8,128)S(1)} %get-tuple-element.7), channel_id=1, source_target_pairs={{0,4},{4,8},{8,12},{12,16},{16,20},{20,24},{24,28},{28,32},{32,36}... | collective-permute-start | bytes 1179656 | tf_op jit(solution)/shard_map/ppermute | solution.py:12
  29.4 12.2 %collective-permute-start.3 = (f32[128,6,1,128]{0,3,2,1:T(8,128)S(1)}, f32[128,6,1,128]{0,3,2,1:T(8,128)S(1)}, u32[]{:S(2)}, u32[]{:S(2)}) collective-permute-start(f32[128,6,1,128]{0,3,2,1:T(8,128)S(1)} %get-tuple-element.8), channel_id=1, source_target_pairs={{4,0},{8,4},{12,8},{16,12},{20,16},{24,20},{28,24},{32,28},{36,32}... | collective-permute-start | bytes 1179656 | tf_op jit(solution)/shard_map/ppermute | solution.py:15
  33.5 8.4 %copy-start.1 = (bf16[256,4,4,128]{3,2,1,0:T(4,128)(2,1)S(1)}, bf16[256,4,4,128]{3,2,1,0:T(4,128)(2,1)}, u32[]{:S(2)}) copy-start(bf16[256,4,4,128]{3,2,1,0:T(4,128)(2,1)} %param.7) | copy-start | bytes 3145732
  41.9 50.7 %copy-start.6 = (f32[256]{0:T(256)S(1)}, f32[256]{0:T(256)}, u32[]{:S(2)}) copy-start(f32[256]{0:T(256)} %param.8) | copy-start | bytes 3076
  92.5 726.8 %all-reduce.7.cloned.1.call-start = ((), (), s32[]{:S(2)}) async-start(), calls=%async_computation.1 | async-start | bytes 262144 | tf_op jit(solution)/shard_map/psum | solution.py:61
  424.8 5.4 collective-permute-start.4
  427.0 7.7 collective-permute-start.5
  434.7 7.8 collective-permute-start.6
  437.4 9.2 %collective-permute-start.7 = (f32[128,6,1,128]{0,3,2,1:T(8,128)S(1)}, f32[128,6,1,128]{0,3,2,1:T(8,128)S(1)}, u32[]{:S(2)}, u32[]{:S(2)}) collective-permute-start(f32[128,6,1,128]{0,3,2,1:T(8,128)S(1)} %get-tuple-element.6), channel_id=1, source_target_pairs={{4,0},{8,4},{12,8},{16,12},{20,16},{24,20},{28,24},{32,28},{36,32}... | collective-permute-start | bytes 1179656 | tf_op jit(solution)/shard_map/ppermute | solution.py:15
  446.9 372.4 %copy-start.2 = (f32[128,256]{1,0:T(8,128)S(1)}, f32[128,256]{1,0:T(8,128)}, u32[]{:S(2)}) copy-start(f32[128,256]{1,0:T(8,128)} %all-reduce.5.cloned.1.call-done) | copy-start | bytes 393220
Sparse Core Ops, SparseCore 0:
  92.6 330.7 all-reduce.4
  497.7 321.5 all-reduce.6
where the time goes:
time: 829 us; the launch traced here: 828 us
  waiting for transfers between devices  674 us (81%)
  matrix products  103 us (12%)
  starting transfers between devices  28.5 us (3%)
  between operations  13.6 us (2%)
    psum x2, waiting for transfers between devices, rate(): modal = lax.psum(partial_sum, ('sy', 'sz'))  653 us
    dot_general x2, matrix products, rate(): lax.dot_general(closure.reshape(batch, rows * depth * width), flat, (((1,...  101 us
    ppermute x4, starting transfers between devices, padded_2(): lax.ppermute(lax.slice_in_dim(block, 0, width, axis=dim), axis, backward)  17.7 us
  transfers between devices with their start and end apart: 10, of which 9 were waited for; matrix products, arithmetic and copies ran while one was open for 0% of the time, Pallas kernels for 0%

commit v1 on v0

v1 whole, which is shorter than its diff:
```python
import functools
import jax
import jax.numpy as jnp
from jax import lax
from jax.experimental import pallas as pl
from jax.experimental.pallas import tpu as pltpu
from jax.sharding import PartitionSpec as P

f32, bf16 = jnp.float32, jnp.bfloat16
MESH = pl.DeviceIdType.MESH
CHUNK = 64


def kernel(
    ny, nz, scale,
    coeffs_ref, damping_ref, w_in, b_in, w_out, basis_hbm,
    out_ref,
    raw, own, halo_y, halo_z, field, left, right, clos,
    state0, state1, result,
    part_f, part_b, in_y, sum_y, in_z, row_out, rows_all, piece,
    raw_sem, halo_send, halo_recv, send_sem, recv_sem,
):
    ns = 2 * ny
    batch, modes = coeffs_ref.shape
    half = modes // 2
    per_y = batch // ny
    per_z = per_y // nz
    sy, sz = lax.axis_index("sy"), lax.axis_index("sz")
    my_y, my_core = sy // 2, lax.rem(sy, 2)

    barrier = pltpu.get_barrier_semaphore()

    def greet_y(d, _):
        pl.semaphore_signal(barrier, inc=1, device_id={"sy": lax.rem(sy + d, ns)}, device_id_type=MESH)
        return 0

    def greet_z(d, _):
        pl.semaphore_signal(barrier, inc=1, device_id={"sz": lax.rem(sz + d, nz)}, device_id_type=MESH)
        return 0

    lax.fori_loop(1, ns, greet_y, 0)
    lax.fori_loop(1, nz, greet_z, 0)

    load = pltpu.make_async_copy(basis_hbm, raw, raw_sem)
    load.start()
    coeffs = coeffs_ref[...]
    state0[0] = coeffs[:, :half].astype(bf16)
    state0[1] = coeffs[:, half:].astype(bf16)
    source = lax.broadcasted_iota(jnp.int32, (256, 256), 1)
    target = lax.broadcasted_iota(jnp.int32, (256, 256), 0)
    perm = jnp.where(
        (lax.shift_right_logical(target, 4) == (source & 15))
        & ((target & 15) == lax.shift_right_logical(source, 4)),
        1.0, 0.0,
    ).astype(bf16)
    load.wait()
    for block in range(16):
        moved = jnp.dot(
            perm, raw[block * 256:(block + 1) * 256, :], preferred_element_type=f32
        ).astype(bf16)
        for cell in range(16):
            own[cell // 4, cell % 4, block * 16:(block + 1) * 16, :] = moved[cell * 16:(cell + 1) * 16]

    pl.semaphore_wait(barrier, ns + nz - 2)

    y_next, y_prev = lax.rem(sy + 1, ns), lax.rem(sy + ns - 1, ns)
    z_next, z_prev = lax.rem(sz + 1, nz), lax.rem(sz + nz - 1, nz)
    halos = []
    for slot, (src, dst, where) in enumerate((
        (own.at[:, 3], halo_z.at[0], {"sz": z_next}),
        (own.at[:, 0], halo_z.at[1], {"sz": z_prev}),
        (own.at[3], halo_y.at[0], {"sy": y_next}),
        (own.at[0], halo_y.at[1], {"sy": y_prev}),
    )):
        copy = pltpu.make_async_remote_copy(
            src_ref=src, dst_ref=dst, send_sem=halo_send.at[slot], recv_sem=halo_recv.at[slot],
            device_id=where, device_id_type=MESH,
        )
        copy.start()
        halos.append(copy)

    def pair_field(state, first, second):
        lhs = jnp.concatenate([state[0], state[1]], axis=1)
        both = jnp.dot(lhs, jnp.concatenate([first, second], axis=1), preferred_element_type=f32)
        return both[:, :128], both[:, 128:]

    lane = lax.broadcasted_iota(jnp.int32, (batch, 128), 1)

    def field_own(state):
        for y in range(4):
            for z in (0, 2):
                for k, value in enumerate(pair_field(state, own[y, z], own[y, z + 1])):
                    field[y + 1, z + k + 1] = value
                    left[y, z + k] = jnp.where(lane == 0, 0.0, pltpu.roll(value, 1, 1))
                    right[y, z + k] = jnp.where(lane == 127, 0.0, pltpu.roll(value, 127, 1))

    def field_y(state):
        for side, inside in ((0, sy > 0), (1, sy < ns - 1)):
            for z in (0, 2):
                for k, value in enumerate(pair_field(state, halo_y[side, z], halo_y[side, z + 1])):
                    field[5 * side, z + k + 1] = jnp.where(inside, value, 0.0)

    def field_z(state):
        for side, inside in ((0, sz > 0), (1, sz < nz - 1)):
            for y in (0, 2):
                for k, value in enumerate(pair_field(state, halo_z[side, y], halo_z[side, y + 1])):
                    field[y + k + 1, 5 * side] = jnp.where(inside, value, 0.0)

    def closure(count, cell_of):
        chunks = batch // CHUNK

        def body(i, _):
            y, z = cell_of(i // chunks)
            at = pl.ds(pl.multiple_of(lax.rem(i, chunks) * CHUNK, CHUNK), CHUNK)
            taps = (
                field[y + 1, z + 1, at, :],
                field[y, z + 1, at, :],
                field[y + 2, z + 1, at, :],
                left[y, z, at, :],
                right[y, z, at, :],
                field[y + 1, z, at, :],
                field[y + 1, z + 2, at, :],
            )
            total = jnp.zeros((CHUNK, 128), f32)
            for h in range(8):
                inner = b_in[h] + w_in[h, 0] * taps[0]
                for k in range(1, 7):
                    inner = inner + w_in[h, k] * taps[k]
                total = total + w_out[h] * jnp.tanh(inner)
            clos[y, z, at, :] = total.astype(bf16)
            return 0

        lax.fori_loop(0, count * chunks, body, 0)

    def project(section):
        lhs = jnp.concatenate([clos[c // 4, c % 4] for c in range(16)], axis=1)
        rhs = jnp.concatenate([own[c // 4, c % 4] for c in range(16)], axis=1)
        partial = lax.dot_general(lhs, rhs, (((1,), (1,)), ((), ())), preferred_element_type=f32)
        for c in range(2):
            part_f[section, c] = partial[:, c * half:(c + 1) * half]
            part_b[section, c] = partial[:, c * half:(c + 1) * half].astype(bf16)

    def exchange(section, phase, axis, count, src_of, dst_of):
        me = sy if axis == "sy" else sz

        def copy_of(d):
            peer = lax.rem(me + d, count)
            return pltpu.make_async_remote_copy(
                src_ref=src_of(peer), dst_ref=dst_of(d),
                send_sem=send_sem.at[section, phase, d], recv_sem=recv_sem.at[section, phase, d],
                device_id={axis: peer}, device_id_type=MESH,
            )

        def start(d, _):
            copy_of(d).start()
            return 0

        def finish(d, _):
            copy_of(d).wait()
            return 0

        lax.fori_loop(1, count, start, 0)
        lax.fori_loop(1, count, finish, 0)

    rows_y = pl.ds(pl.multiple_of(my_y * per_y, per_y), per_y)

    def reduced(section):
        exchange(
            section, 0, "sy", ns,
            lambda t: part_b.at[section, lax.rem(t, 2), pl.ds(pl.multiple_of(t // 2 * per_y, per_y), per_y)],
            lambda d: in_y.at[section, d],
        )
        total = part_f[section, my_core, rows_y, :]
        for d in range(1, ns):
            total = total + in_y[section, d].astype(f32)
        for z in range(nz):
            sum_y[section, z] = total[z * per_z:(z + 1) * per_z]
        exchange(
            section, 1, "sz", nz,
            lambda t: sum_y.at[section, t],
            lambda d: in_z.at[section, d],
        )
        modal = sum_y[section, sz]
        for d in range(1, nz):
            modal = modal + in_z[section, d]
        return modal

    def spread(section, rows, whole):
        row_out[section] = rows
        exchange(
            section, 2, "sz", nz,
            lambda t: row_out.at[section],
            lambda d: rows_all.at[section, sz],
        )
        rows_all[section, sz] = rows
        block = jnp.concatenate([rows_all[section, z] for z in range(nz)], axis=0).astype(bf16)
        piece[section] = block
        exchange(
            section, 3, "sy", ns,
            lambda t: piece.at[section],
            lambda d: whole.at[my_core, rows_y],
        )
        whole[my_core, rows_y, :] = block

    damping = damping_ref[pl.ds(my_core, 1), :]
    both_halves = coeffs_ref[pl.ds(my_y * per_y + sz * per_z, per_z), :]
    my_rows = jnp.where(my_core == 0, both_halves[:, :half], both_halves[:, half:])

    field_own(state0)
    closure(4, lambda i: (1 + i // 2, 1 + lax.rem(i, 2)))
    halos[2].wait()
    halos[3].wait()
    field_y(state0)
    closure(4, lambda i: (i // 2 * 3, 1 + lax.rem(i, 2)))
    halos[0].wait()
    halos[1].wait()
    field_z(state0)
    closure(8, lambda i: (i // 2, lax.rem(i, 2) * 3))
    project(0)
    first = scale * reduced(0) - damping * my_rows
    middle = my_rows + 0.5 * first
    spread(0, middle, state1)

    field_own(state1)
    field_y(state1)
    field_z(state1)
    closure(16, lambda i: (i // 4, lax.rem(i, 4)))
    project(1)
    second = scale * reduced(1) - damping * middle
    spread(1, 0.5 * (first + second), result)
    out_ref[...] = jnp.concatenate([result[0], result[1]], axis=1).astype(f32)


def local(coeffs, basis, damping, w_in, b_in, w_out):
    batch = coeffs.shape[0]
    modes, rows, depth, width = basis.shape
    ns, nz = lax.axis_size("sy"), lax.axis_size("sz")
    ny = ns // 2
    half = modes // 2
    per_y = batch // ny
    per_z = per_y // nz
    scale = (modes / (rows * depth * width * ns * nz)) ** 0.5
    vmem, smem = pl.BlockSpec(memory_space=pltpu.VMEM), pl.BlockSpec(memory_space=pltpu.SMEM)
    return pl.pallas_call(
        functools.partial(kernel, ny, nz, scale),
        out_shape=jax.ShapeDtypeStruct((batch, modes), f32),
        in_specs=[vmem, vmem, smem, smem, smem, pl.BlockSpec(memory_space=pl.ANY)],
        out_specs=vmem,
        scratch_shapes=[
            pltpu.VMEM((modes * rows * depth, width), bf16),
            pltpu.VMEM((rows, depth, modes, width), bf16),
            pltpu.VMEM((2, depth, modes, width), bf16),
            pltpu.VMEM((2, rows, modes, width), bf16),
            pltpu.VMEM((rows + 2, depth + 2, batch, width), f32),
            pltpu.VMEM((rows, depth, batch, width), f32),
            pltpu.VMEM((rows, depth, batch, width), f32),
            pltpu.VMEM((rows, depth, batch, width), bf16),
            pltpu.VMEM((2, batch, half), bf16),
            pltpu.VMEM((2, batch, half), bf16),
            pltpu.VMEM((2, batch, half), bf16),
            pltpu.VMEM((2, 2, batch, half), f32),
            pltpu.VMEM((2, 2, batch, half), bf16),
            pltpu.VMEM((2, ns, per_y, half), bf16),
            pltpu.VMEM((2, nz, per_z, half), f32),
            pltpu.VMEM((2, nz, per_z, half), f32),
            pltpu.VMEM((2, per_z, half), f32),
            pltpu.VMEM((2, nz, per_z, half), f32),
            pltpu.VMEM((2, per_y, half), bf16),
            pltpu.SemaphoreType.DMA,
            pltpu.SemaphoreType.DMA((4,)),
            pltpu.SemaphoreType.DMA((4,)),
            pltpu.SemaphoreType.DMA((2, 4, 16)),
            pltpu.SemaphoreType.DMA((2, 4, 16)),
        ],
        compiler_params=pltpu.CompilerParams(
            collective_id=0, has_side_effects=True, vmem_limit_bytes=32 << 20
        ),
        cost_estimate=pl.CostEstimate(
            flops=2_000_000_000, bytes_accessed=1_500_000, transcendentals=4_194_304
        ),
    )(
        coeffs, damping.reshape(2, half), w_in, b_in, w_out,
        basis.reshape(modes * rows * depth, width),
    )


def solution(mesh):
    return jax.shard_map(
        local,
        mesh=mesh,
        in_specs=(P("traj", None), P(None, "sy", "sz", None), P(), P(), P(), P()),
        out_specs=P("traj", None),
        check_vma=False,
    )
```

time: 829 us -> 98 us (0.12)
  waiting for transfers between devices: 674 us -> 0 us
  matrix products: 103 us -> 0 us
  Pallas kernels: 0 us -> 93.6 us
  starting transfers between devices: 28.5 us -> 0 us
  between operations: 13.6 us -> 0.02 us
    psum x2 -> x0, waiting for transfers between devices: 653 us -> none  [rate(): modal = lax.psum(partial_sum, ('sy', 'sz'))]
    dot_general x4 -> x0, matrix products: 103 us -> none  [the longest x2 101 us: rate(): lax.dot_general(closure.reshape(batch, rows * depth * width), flat, (((1,...]
    pallas_call x0 -> x1, Pallas kernels: none -> 93.6 us  [local(): pl.pallas_call(functools.partial(kernel, ny, nz, scale), out_shape=jax.Sh...]
    ppermute x8 -> x0, starting transfers between devices: 28.5 us -> none  [the longest x4 17.7 us: padded_2(): lax.ppermute(lax.slice_in_dim(block, 0, width, axis=dim), axis, backward)]
    ppermute x8 -> x0, waiting for transfers between devices: 21.8 us -> none  [the longest x4 12.8 us: padded_2(): lax.ppermute(lax.slice_in_dim(block, 0, width, axis=dim), axis, backward)]
  transfers between devices with their start and end apart: 10 -> 0, of which waited for: 9 -> 0; matrix products, arithmetic and copies ran while one was open for 0% -> 0% of each run, Pallas kernels for 0% -> 0%
where the time goes in v1:
time: 98 us; the launch traced here: 97.8 us
  Pallas kernels  93.6 us (96%)
  local copies, waits for them, and re-layouts  4.16 us (4%)
    pallas_call x1, Pallas kernels, local(): pl.pallas_call(functools.partial(kernel, ny, nz, scale), out_shape=jax.Sh...  93.6 us
    unnamed x13, local copies, waits for them, and re-layouts  4.16 us

profile of v1, /device:TPU:1, one launch (start us, length us, event | category | flops | bytes accessed | tf_op | source)
XLA Modules:
  0.0 97.8 jit_solution(8640968970405045456)
XLA Ops:
  0.0 0.0 copy-start.5
  0.0 0.0 copy-start.3
  0.0 0.0 copy-start.4
  0.0 0.6 copy-done.5
  0.7 0.0 copy-done.3
  0.7 0.0 copy-done.4
  0.7 0.0 copy-start
  0.7 1.2 %copy-done = bf16[256,4,4,128]{3,2,1,0:T(4,128)(2,1)S(1)} copy-done((bf16[256,4,4,128]{3,2,1,0:T(4,128)(2,1)S(1)}, bf16[256,4,4,128]{3,2,1,0:T(4,128)(2,1)}, u32[]{:S(2)}) %copy-start) | copy-done | bytes 1048600
  1.9 0.0 copy-start.1
  1.9 0.9 copy-done.1
  2.8 0.0 copy-start.2
  2.8 0.7 copy-done.2
  3.5 93.6 %shard_map.64 = f32[128,256]{1,0:T(8,128)S(1)} custom-call(f32[128,256]{1,0:T(8,128)S(1)} %copy-done.1, f32[2,128]{1,0:T(2,128)S(1)} %bitcast.3, f32[8,7]{1,0:T(8,128)S(1)} %copy-done.2, f32[8]{0:T(128)S(1)} %copy-done.4, f32[8]{0:T(128)S(1)} %copy-done.5, bf16[4096,128]{1,0:T(8,128)(2,1)S(1)} %bitcast.2), custom_call_target="tpu_custom_call" | custom-call | flops 2000000000 | bytes 1500000 | tf_op jit(solution)/shard_map/pallas_call | solution.py:244
  97.1 0.7 copy.8
Async XLA Ops:
  0.0 0.7 copy-start.5
  0.0 0.7 copy-start.3
  0.0 0.7 copy-start.4
  0.7 1.2 %copy-start = (bf16[256,4,4,128]{3,2,1,0:T(4,128)(2,1)S(1)}, bf16[256,4,4,128]{3,2,1,0:T(4,128)(2,1)}, u32[]{:S(2)}) copy-start(bf16[256,4,4,128]{3,2,1,0:T(4,128)(2,1)} %param.7) | copy-start | bytes 3145732
  1.9 0.9 copy-start.1
  2.8 0.7 copy-start.2

commit v2 on v1

--- a/solution.py
+++ b/solution.py
@@ -8,27 +8,39 @@
 
 f32, bf16 = jnp.float32, jnp.bfloat16
 MESH = pl.DeviceIdType.MESH
-CHUNK = 64
+CHUNK = 128
 
 
 def kernel(
     ny, nz, scale,
-    coeffs_ref, damping_ref, w_in, b_in, w_out, basis_hbm,
+    coeffs_hbm, damping_hbm, w_in_hbm, b_in_hbm, w_out_hbm, basis_hbm,
     out_ref,
     raw, own, halo_y, halo_z, field, left, right, clos,
     state0, state1, result,
-    part_f, part_b, in_y, sum_y, in_z, row_out, rows_all, piece,
-    raw_sem, halo_send, halo_recv, send_sem, recv_sem,
+    part_f, part_b, in_y, sum_y, in_z, piece,
+    coeffs_ref, damping_ref, w_in, b_in, w_out,
+    raw_sem, small_sem, halo_send, halo_recv, send_sem, recv_sem,
 ):
     ns = 2 * ny
-    batch, modes = coeffs_ref.shape
+    batch, modes = coeffs_hbm.shape
     half = modes // 2
     per_y = batch // ny
-    per_z = per_y // nz
     sy, sz = lax.axis_index("sy"), lax.axis_index("sz")
     my_y, my_core = sy // 2, lax.rem(sy, 2)
 
     barrier = pltpu.get_barrier_semaphore()
+
+    load = pltpu.make_async_copy(basis_hbm, raw, raw_sem)
+    load.start()
+    small = [
+        pltpu.make_async_copy(src, dst, small_sem.at[i])
+        for i, (src, dst) in enumerate((
+            (coeffs_hbm, coeffs_ref), (damping_hbm, damping_ref),
+            (w_in_hbm, w_in), (b_in_hbm, b_in), (w_out_hbm, w_out),
+        ))
+    ]
+    for copy in small:
+        copy.start()
 
     def greet_y(d, _):
         pl.semaphore_signal(barrier, inc=1, device_id={"sy": lax.rem(sy + d, ns)}, device_id_type=MESH)
@@ -41,8 +53,8 @@
     lax.fori_loop(1, ns, greet_y, 0)
     lax.fori_loop(1, nz, greet_z, 0)
 
-    load = pltpu.make_async_copy(basis_hbm, raw, raw_sem)
-    load.start()
+    for copy in small:
+        copy.wait()
     coeffs = coeffs_ref[...]
     state0[0] = coeffs[:, :half].astype(bf16)
     state0[1] = coeffs[:, half:].astype(bf16)
@@ -142,68 +154,60 @@
 
     def exchange(section, phase, axis, count, src_of, dst_of):
         me = sy if axis == "sy" else sz
-
-        def copy_of(d):
+        copies = []
+        for d in sorted(range(1, count), key=lambda d: -min(d, count - d)):
             peer = lax.rem(me + d, count)
-            return pltpu.make_async_remote_copy(
+            copy = pltpu.make_async_remote_copy(
                 src_ref=src_of(peer), dst_ref=dst_of(d),
                 send_sem=send_sem.at[section, phase, d], recv_sem=recv_sem.at[section, phase, d],
                 device_id={axis: peer}, device_id_type=MESH,
             )
-
-        def start(d, _):
-            copy_of(d).start()
-            return 0
-
-        def finish(d, _):
-            copy_of(d).wait()
-            return 0
-
-        lax.fori_loop(1, count, start, 0)
-        lax.fori_loop(1, count, finish, 0)
+            copy.start()
+            copies.append(copy)
+        return copies
 
     rows_y = pl.ds(pl.multiple_of(my_y * per_y, per_y), per_y)
 
     def reduced(section):
-        exchange(
+        copies = exchange(
             section, 0, "sy", ns,
             lambda t: part_b.at[section, lax.rem(t, 2), pl.ds(pl.multiple_of(t // 2 * per_y, per_y), per_y)],
             lambda d: in_y.at[section, d],
         )
+        for copy in copies:
+            copy.wait()
         total = part_f[section, my_core, rows_y, :]
         for d in range(1, ns):
             total = total + in_y[section, d].astype(f32)
-        for z in range(nz):
-            sum_y[section, z] = total[z * per_z:(z + 1) * per_z]
-        exchange(
+        total = total.astype(bf16)
+        sum_y[section] = total
+        copies = exchange(
             section, 1, "sz", nz,
-            lambda t: sum_y.at[section, t],
-            lambda d: in_z.at[section, d],
+            lambda t: sum_y.at[section],
+            lambda d: in_z.at[section, sz],
         )
-        modal = sum_y[section, sz]
-        for d in range(1, nz):
-            modal = modal + in_z[section, d]
+        in_z[section, sz] = total
+        for copy in copies:
+            copy.wait()
+        modal = in_z[section, 0].astype(f32)
+        for z in range(1, nz):
+            modal = modal + in_z[section, z].astype(f32)
         return modal
 
     def spread(section, rows, whole):
-        row_out[section] = rows
-        exchange(
-            section, 2, "sz", nz,
-            lambda t: row_out.at[section],
-            lambda d: rows_all.at[section, sz],
-        )
-        rows_all[section, sz] = rows
-        block = jnp.concatenate([rows_all[section, z] for z in range(nz)], axis=0).astype(bf16)
+        block = rows.astype(bf16)
         piece[section] = block
-        exchange(
-            section, 3, "sy", ns,
+        copies = exchange(
+            section, 2, "sy", ns,
             lambda t: piece.at[section],
             lambda d: whole.at[my_core, rows_y],
         )
         whole[my_core, rows_y, :] = block
+        for copy in copies:
+            copy.wait()
 
     damping = damping_ref[pl.ds(my_core, 1), :]
-    both_halves = coeffs_ref[pl.ds(my_y * per_y + sz * per_z, per_z), :]
+    both_halves = coeffs_ref[rows_y, :]
     my_rows = jnp.where(my_core == 0, both_halves[:, :half], both_halves[:, half:])
 
     field_own(state0)
@@ -238,14 +242,12 @@
     ny = ns // 2
     half = modes // 2
     per_y = batch // ny
-    per_z = per_y // nz
     scale = (modes / (rows * depth * width * ns * nz)) ** 0.5
-    vmem, smem = pl.BlockSpec(memory_space=pltpu.VMEM), pl.BlockSpec(memory_space=pltpu.SMEM)
     return pl.pallas_call(
         functools.partial(kernel, ny, nz, scale),
         out_shape=jax.ShapeDtypeStruct((batch, modes), f32),
-        in_specs=[vmem, vmem, smem, smem, smem, pl.BlockSpec(memory_space=pl.ANY)],
-        out_specs=vmem,
+        in_specs=[pl.BlockSpec(memory_space=pltpu.HBM)] * 6,
+        out_specs=pl.BlockSpec(memory_space=pltpu.VMEM),
         scratch_shapes=[
             pltpu.VMEM((modes * rows * depth, width), bf16),
             pltpu.VMEM((rows, depth, modes, width), bf16),
@@ -261,19 +263,23 @@
             pltpu.VMEM((2, 2, batch, half), f32),
             pltpu.VMEM((2, 2, batch, half), bf16),
             pltpu.VMEM((2, ns, per_y, half), bf16),
-            pltpu.VMEM((2, nz, per_z, half), f32),
-            pltpu.VMEM((2, nz, per_z, half), f32),
-            pltpu.VMEM((2, per_z, half), f32),
-            pltpu.VMEM((2, nz, per_z, half), f32),
             pltpu.VMEM((2, per_y, half), bf16),
+            pltpu.VMEM((2, nz, per_y, half), bf16),
+            pltpu.VMEM((2, per_y, half), bf16),
+            pltpu.VMEM((batch, modes), f32),
+            pltpu.VMEM((2, half), f32),
+            pltpu.SMEM((8, 7), f32),
+            pltpu.SMEM((8,), f32),
+            pltpu.SMEM((8,), f32),
             pltpu.SemaphoreType.DMA,
+            pltpu.SemaphoreType.DMA((5,)),
             pltpu.SemaphoreType.DMA((4,)),
             pltpu.SemaphoreType.DMA((4,)),
-            pltpu.SemaphoreType.DMA((2, 4, 16)),
-            pltpu.SemaphoreType.DMA((2, 4, 16)),
+            pltpu.SemaphoreType.DMA((2, 3, 16)),
+            pltpu.SemaphoreType.DMA((2, 3, 16)),
         ],
         compiler_params=pltpu.CompilerParams(
-            collective_id=0, has_side_effects=True, vmem_limit_bytes=32 << 20
+            collective_id=0, has_side_effects=True, vmem_limit_bytes=60 << 20
         ),
         cost_estimate=pl.CostEstimate(
             flops=2_000_000_000, bytes_accessed=1_500_000, transcendentals=4_194_304

time: 98 us -> 77.7 us (0.79)
  Pallas kernels: 93.6 us -> 75.9 us
  local copies, waits for them, and re-layouts: 4.16 us -> 1.57 us
    pallas_call x1, Pallas kernels: 93.6 us -> 75.9 us  [local(): pl.pallas_call(functools.partial(kernel, ny, nz, scale), out_shape=jax.Sh...]
    unnamed x13 -> x1, local copies, waits for them, and re-layouts: 4.16 us -> 1.57 us
where the time goes in v2:
time: 77.7 us; the launch traced here: 77.5 us
  Pallas kernels  75.9 us (98%)
  local copies, waits for them, and re-layouts  1.57 us (2%)
    pallas_call x1, Pallas kernels, local(): pl.pallas_call(functools.partial(kernel, ny, nz, scale), out_shape=jax.Sh...  75.9 us
    unnamed x1, local copies, waits for them, and re-layouts  1.57 us

profile of v2, /device:TPU:1, one launch (start us, length us, event | category | flops | bytes accessed | tf_op | source)
XLA Modules:
  0.0 77.5 jit_solution(9042608096147372806)
XLA Ops:
  0.0 75.9 %shard_map.64 = f32[128,256]{1,0:T(8,128)} custom-call(f32[128,256]{1,0:T(8,128)} %coeffs_hbm.1, f32[2,128]{1,0:T(2,128)} %bitcast.3, f32[8,7]{1,0:T(8,128)} %w_in_hbm.1, f32[8]{0:T(128)} %b_in_hbm.1, f32[8]{0:T(128)} %w_out_hbm.1, bf16[4096,128]{1,0:T(8,128)(2,1)} %bitcast.2), custom_call_target="tpu_custom_call" | custom-call | flops 2000000000 | bytes 1500000 | tf_op jit(solution)/shard_map/pallas_call | solution.py:246
  75.9 1.6 %copy.8 = f32[128,256]{1,0:T(8,128)} copy(f32[128,256]{1,0:T(8,128)} %shard_map.64) | data formatting | bytes 262144

commit v3 on v2

--- a/solution.py
+++ b/solution.py
@@ -8,18 +8,20 @@
 
 f32, bf16 = jnp.float32, jnp.bfloat16
 MESH = pl.DeviceIdType.MESH
-CHUNK = 128
+GROUP = 4
+SUM_TYPE = bf16
 
 
 def kernel(
     ny, nz, scale,
     coeffs_hbm, damping_hbm, w_in_hbm, b_in_hbm, w_out_hbm, basis_hbm,
     out_ref,
-    raw, own, halo_y, halo_z, field, left, right, clos,
+    raw, own, halo_y, halo_z, field, field_b, clos, weights, turned,
+    edge_y, edge_z, next_y, next_z,
     state0, state1, result,
     part_f, part_b, in_y, sum_y, in_z, piece,
     coeffs_ref, damping_ref, w_in, b_in, w_out,
-    raw_sem, small_sem, halo_send, halo_recv, send_sem, recv_sem,
+    raw_sem, small_sem, halo_send, halo_recv, edge_send, edge_recv, send_sem, recv_sem,
 ):
     ns = 2 * ny
     batch, modes = coeffs_hbm.shape
@@ -77,80 +79,156 @@
 
     y_next, y_prev = lax.rem(sy + 1, ns), lax.rem(sy + ns - 1, ns)
     z_next, z_prev = lax.rem(sz + 1, nz), lax.rem(sz + nz - 1, nz)
-    halos = []
-    for slot, (src, dst, where) in enumerate((
-        (own.at[:, 3], halo_z.at[0], {"sz": z_next}),
-        (own.at[:, 0], halo_z.at[1], {"sz": z_prev}),
-        (own.at[3], halo_y.at[0], {"sy": y_next}),
-        (own.at[0], halo_y.at[1], {"sy": y_prev}),
-    )):
-        copy = pltpu.make_async_remote_copy(
-            src_ref=src, dst_ref=dst, send_sem=halo_send.at[slot], recv_sem=halo_recv.at[slot],
-            device_id=where, device_id_type=MESH,
+    sides = (({"sz": z_next}, {"sz": z_prev}), ({"sy": y_next}, {"sy": y_prev}))
+
+    def remote(src, dst, send, recv, where):
+        return pltpu.make_async_remote_copy(
+            src_ref=src, dst_ref=dst, send_sem=send, recv_sem=recv, device_id=where, device_id_type=MESH
         )
-        copy.start()
-        halos.append(copy)
+
+    def basis_halo(dim):
+        faces = ((own.at[:, 3], own.at[:, 0]), (own.at[3], own.at[0]))[dim]
+        copies = [
+            remote(
+                faces[side], (halo_z, halo_y)[dim].at[side],
+                halo_send.at[dim, side], halo_recv.at[dim, side], sides[dim][side],
+            )
+            for side in range(2)
+        ]
+        for copy in copies:
+            copy.start()
+        return copies
+
+    chunks = ns // GROUP
+    chunk_rows = batch // chunks
+    order = sorted(range(chunks), key=lambda o: (-min(o, chunks - o), o))
+    my_chunk, my_place = sy // GROUP, lax.rem(sy, GROUP)
+
+    def chunk_of(offset):
+        chunk = lax.rem(my_chunk + offset, chunks)
+        return chunk, pl.ds(pl.multiple_of(chunk * chunk_rows, chunk_rows), chunk_rows)
+
+    def edge_copies(offset):
+        chunk, at = chunk_of(offset)
+        return [
+            remote(
+                (edge_z, edge_y)[dim].at[side, :, at], (next_z, next_y)[dim].at[side, :, at],
+                edge_send.at[dim, side, chunk], edge_recv.at[dim, side, chunk], sides[dim][side],
+            )
+            for dim in range(2) for side in range(2)
+        ]
 
     def pair_field(state, first, second):
         lhs = jnp.concatenate([state[0], state[1]], axis=1)
         both = jnp.dot(lhs, jnp.concatenate([first, second], axis=1), preferred_element_type=f32)
         return both[:, :128], both[:, 128:]
 
-    lane = lax.broadcasted_iota(jnp.int32, (batch, 128), 1)
-
-    def field_own(state):
+    def put(y, z, at, value):
+        field[y, z, at, :] = value
+        if y < 5 and 0 < z < 5:
+            field_b[y, z - 1, at, :] = value.astype(bf16)
+
+    everything = slice(None)
+
+    def field_own(state, edges):
         for y in range(4):
             for z in (0, 2):
                 for k, value in enumerate(pair_field(state, own[y, z], own[y, z + 1])):
-                    field[y + 1, z + k + 1] = value
-                    left[y, z + k] = jnp.where(lane == 0, 0.0, pltpu.roll(value, 1, 1))
-                    right[y, z + k] = jnp.where(lane == 127, 0.0, pltpu.roll(value, 127, 1))
+                    put(y + 1, z + k + 1, everything, value)
+                    if edges and y in (0, 3):
+                        edge_y[int(y == 0), z + k] = value.astype(bf16)
+                    if edges and z + k in (0, 3):
+                        edge_z[int(z + k == 0), y] = value.astype(bf16)
 
     def field_y(state):
         for side, inside in ((0, sy > 0), (1, sy < ns - 1)):
             for z in (0, 2):
                 for k, value in enumerate(pair_field(state, halo_y[side, z], halo_y[side, z + 1])):
-                    field[5 * side, z + k + 1] = jnp.where(inside, value, 0.0)
+                    put(5 * side, z + k + 1, everything, jnp.where(inside, value, 0.0))
 
     def field_z(state):
         for side, inside in ((0, sz > 0), (1, sz < nz - 1)):
             for y in (0, 2):
                 for k, value in enumerate(pair_field(state, halo_z[side, y], halo_z[side, y + 1])):
-                    field[y + k + 1, 5 * side] = jnp.where(inside, value, 0.0)
-
-    def closure(count, cell_of):
-        chunks = batch // CHUNK
+                    put(y + k + 1, 5 * side, everything, jnp.where(inside, value, 0.0))
+
+    def edges_in(at):
+        for side, inside in ((0, sy > 0), (1, sy < ns - 1)):
+            for z in range(4):
+                put(5 * side, z + 1, at, jnp.where(inside, next_y[side, z, at, :].astype(f32), 0.0))
+        for side, inside in ((0, sz > 0), (1, sz < nz - 1)):
+            for y in range(4):
+                put(y + 1, 5 * side, at, jnp.where(inside, next_z[side, y, at, :].astype(f32), 0.0))
+
+    def build_weights():
+        row = lax.broadcasted_iota(jnp.int32, (128, 128), 0)
+        col = lax.broadcasted_iota(jnp.int32, (128, 128), 1)
+        for h in range(8):
+            band = jnp.where(row == col, w_in[h, 0], 0.0)
+            band = jnp.where(row + 1 == col, w_in[h, 3], band)
+            band = jnp.where(row == col + 1, w_in[h, 4], band)
+            for block, value in enumerate((band, jnp.where(row == col, w_in[h, 1], 0.0))):
+                high = value.astype(bf16)
+                low = (value - high.astype(f32)).astype(bf16)
+                for part, kept in enumerate((high, low)):
+                    at = (2 * part + block) * 128
+                    weights[at:at + 128, h * 128:(h + 1) * 128] = kept
+
+    def closure(at):
+        stack = 128 // chunk_rows
 
         def body(i, _):
-            y, z = cell_of(i // chunks)
-            at = pl.ds(pl.multiple_of(lax.rem(i, chunks) * CHUNK, CHUNK), CHUNK)
+            cells = [((i * stack + j) // 4, lax.rem(i * stack + j, 4)) for j in range(stack)]
+
+            def stacked(take):
+                return jnp.concatenate([take(y, z) for y, z in cells], axis=0)
+
+            near = stacked(lambda y, z: jnp.concatenate(
+                [field_b[y + 1, z, at, :], field_b[y, z, at, :]], axis=1
+            ))
+            near = jnp.concatenate([near, near], axis=1)
             taps = (
-                field[y + 1, z + 1, at, :],
-                field[y, z + 1, at, :],
-                field[y + 2, z + 1, at, :],
-                left[y, z, at, :],
-                right[y, z, at, :],
-                field[y + 1, z, at, :],
-                field[y + 1, z + 2, at, :],
-            )
-            total = jnp.zeros((CHUNK, 128), f32)
-            for h in range(8):
-                inner = b_in[h] + w_in[h, 0] * taps[0]
-                for k in range(1, 7):
-                    inner = inner + w_in[h, k] * taps[k]
-                total = total + w_out[h] * jnp.tanh(inner)
-            clos[y, z, at, :] = total.astype(bf16)
+                (2, stacked(lambda y, z: field[y + 2, z + 1, at, :])),
+                (5, stacked(lambda y, z: field[y + 1, z, at, :])),
+                (6, stacked(lambda y, z: field[y + 1, z + 2, at, :])),
+            )
+            total = jnp.zeros((stack * chunk_rows, 128), f32)
+            for pair in range(4):
+                both = jnp.dot(
+                    near, weights[:, pair * 256:(pair + 1) * 256], preferred_element_type=f32
+                )
+                for k in range(2):
+                    h = 2 * pair + k
+                    inner = both[:, k * 128:(k + 1) * 128] + b_in[h]
+                    for index, tap in taps:
+                        inner = inner + w_in[h, index] * tap
+                    total = total + w_out[h] * jnp.tanh(inner)
+            for j, (y, z) in enumerate(cells):
+                clos[y, z, at, :] = total[j * chunk_rows:(j + 1) * chunk_rows].astype(bf16)
             return 0
 
-        lax.fori_loop(0, count * chunks, body, 0)
-
-    def project(section):
-        lhs = jnp.concatenate([clos[c // 4, c % 4] for c in range(16)], axis=1)
-        rhs = jnp.concatenate([own[c // 4, c % 4] for c in range(16)], axis=1)
-        partial = lax.dot_general(lhs, rhs, (((1,), (1,)), ((), ())), preferred_element_type=f32)
+        lax.fori_loop(0, 16 // stack, body, 0, unroll=4)
+
+    def project(section, offset):
+        chunk, at = chunk_of(offset)
+        lhs = jnp.concatenate([clos[c // 4, c % 4, at, :] for c in range(16)], axis=1)
+        partial = jnp.dot(lhs, turned[...], preferred_element_type=f32)
         for c in range(2):
-            part_f[section, c] = partial[:, c * half:(c + 1) * half]
-            part_b[section, c] = partial[:, c * half:(c + 1) * half].astype(bf16)
+            part_f[section, c, at, :] = partial[:, c * half:(c + 1) * half]
+            part_b[section, c, at, :] = partial[:, c * half:(c + 1) * half].astype(bf16)
+        copies = []
+        for i in range(int(offset == 0), GROUP):
+            place = lax.rem(my_place + i, GROUP) if offset == 0 else i
+            target = chunk * GROUP + place
+            ahead = lax.rem(target + ns - sy, ns)
+            copy = remote(
+                part_b.at[section, lax.rem(target, 2), pl.ds(pl.multiple_of(target // 2 * per_y, per_y), per_y)],
+                in_y.at[section, ahead],
+                send_sem.at[section, 0, offset * GROUP + i], recv_sem.at[section, 0, ahead], {"sy": target},
+            )
+            copy.start()
+            copies.append(copy)
+        return copies
 
     def exchange(section, phase, axis, count, src_of, dst_of):
         me = sy if axis == "sy" else sz
@@ -169,30 +247,29 @@
     rows_y = pl.ds(pl.multiple_of(my_y * per_y, per_y), per_y)
 
     def reduced(section):
-        copies = exchange(
-            section, 0, "sy", ns,
-            lambda t: part_b.at[section, lax.rem(t, 2), pl.ds(pl.multiple_of(t // 2 * per_y, per_y), per_y)],
-            lambda d: in_y.at[section, d],
-        )
-        for copy in copies:
-            copy.wait()
+        for d in range(1, ns):
+            remote(
+                piece.at[section], in_y.at[section, d],
+                send_sem.at[section, 0, d], recv_sem.at[section, 0, d], {"sy": lax.rem(sy + d, ns)},
+            ).wait_recv()
         total = part_f[section, my_core, rows_y, :]
         for d in range(1, ns):
             total = total + in_y[section, d].astype(f32)
-        total = total.astype(bf16)
+        total = total.astype(SUM_TYPE)
         sum_y[section] = total
         copies = exchange(
             section, 1, "sz", nz,
             lambda t: sum_y.at[section],
             lambda d: in_z.at[section, sz],
         )
+        between = basis_halo(1) if section == 0 else []
         in_z[section, sz] = total
         for copy in copies:
             copy.wait()
         modal = in_z[section, 0].astype(f32)
         for z in range(1, nz):
             modal = modal + in_z[section, z].astype(f32)
-        return modal
+        return modal, between
 
     def spread(section, rows, whole):
         block = rows.astype(bf16)
@@ -210,28 +287,42 @@
     both_halves = coeffs_ref[rows_y, :]
     my_rows = jnp.where(my_core == 0, both_halves[:, :half], both_halves[:, half:])
 
-    field_own(state0)
-    closure(4, lambda i: (1 + i // 2, 1 + lax.rem(i, 2)))
-    halos[2].wait()
-    halos[3].wait()
-    field_y(state0)
-    closure(4, lambda i: (i // 2 * 3, 1 + lax.rem(i, 2)))
-    halos[0].wait()
-    halos[1].wait()
-    field_z(state0)
-    closure(8, lambda i: (i // 2, lax.rem(i, 2) * 3))
-    project(0)
-    first = scale * reduced(0) - damping * my_rows
+    field_own(state0, True)
+    edges = [edge_copies(offset) for offset in order]
+    for group in edges:
+        for copy in group:
+            copy.start()
+    build_weights()
+    for cell in range(16):
+        turned[cell * 128:(cell + 1) * 128, :] = own[cell // 4, cell % 4].T
+    sent = []
+    for step, offset in enumerate(order):
+        for copy in edges[step]:
+            copy.wait_recv()
+        if step == min(1, chunks - 1):
+            halo = basis_halo(0)
+        edges_in(chunk_of(offset)[1])
+        closure(chunk_of(offset)[1])
+        sent += project(0, offset)
+    modal, more = reduced(0)
+    halo += more
+    first = scale * modal - damping * my_rows
     middle = my_rows + 0.5 * first
     spread(0, middle, state1)
 
-    field_own(state1)
+    field_own(state1, False)
+    for copy in halo:
+        copy.wait()
     field_y(state1)
     field_z(state1)
-    closure(16, lambda i: (i // 4, lax.rem(i, 4)))
-    project(1)
-    second = scale * reduced(1) - damping * middle
+    for offset in order:
+        closure(chunk_of(offset)[1])
+        sent += project(1, offset)
+    modal, _ = reduced(1)
+    second = scale * modal - damping * middle
     spread(1, 0.5 * (first + second), result)
+    for copy in sum(edges, sent):
+        copy.wait_send()
     out_ref[...] = jnp.concatenate([result[0], result[1]], axis=1).astype(f32)
 
 
@@ -254,17 +345,22 @@
             pltpu.VMEM((2, depth, modes, width), bf16),
             pltpu.VMEM((2, rows, modes, width), bf16),
             pltpu.VMEM((rows + 2, depth + 2, batch, width), f32),
-            pltpu.VMEM((rows, depth, batch, width), f32),
-            pltpu.VMEM((rows, depth, batch, width), f32),
+            pltpu.VMEM((rows + 1, depth, batch, width), bf16),
             pltpu.VMEM((rows, depth, batch, width), bf16),
+            pltpu.VMEM((512, 1024), bf16),
+            pltpu.VMEM((rows * depth * width, modes), bf16),
+            pltpu.VMEM((2, depth, batch, width), bf16),
+            pltpu.VMEM((2, rows, batch, width), bf16),
+            pltpu.VMEM((2, depth, batch, width), bf16),
+            pltpu.VMEM((2, rows, batch, width), bf16),
             pltpu.VMEM((2, batch, half), bf16),
             pltpu.VMEM((2, batch, half), bf16),
             pltpu.VMEM((2, batch, half), bf16),
             pltpu.VMEM((2, 2, batch, half), f32),
             pltpu.VMEM((2, 2, batch, half), bf16),
             pltpu.VMEM((2, ns, per_y, half), bf16),
-            pltpu.VMEM((2, per_y, half), bf16),
-            pltpu.VMEM((2, nz, per_y, half), bf16),
+            pltpu.VMEM((2, per_y, half), SUM_TYPE),
+            pltpu.VMEM((2, nz, per_y, half), SUM_TYPE),
             pltpu.VMEM((2, per_y, half), bf16),
             pltpu.VMEM((batch, modes), f32),
             pltpu.VMEM((2, half), f32),
@@ -273,8 +369,10 @@
             pltpu.SMEM((8,), f32),
             pltpu.SemaphoreType.DMA,
             pltpu.SemaphoreType.DMA((5,)),
-            pltpu.SemaphoreType.DMA((4,)),
-            pltpu.SemaphoreType.DMA((4,)),
+            pltpu.SemaphoreType.DMA((2, 2)),
+            pltpu.SemaphoreType.DMA((2, 2)),
+            pltpu.SemaphoreType.DMA((2, 2, ns // GROUP)),
+            pltpu.SemaphoreType.DMA((2, 2, ns // GROUP)),
             pltpu.SemaphoreType.DMA((2, 3, 16)),
             pltpu.SemaphoreType.DMA((2, 3, 16)),
         ],

time: 77.7 us -> 72.4 us (0.932)
  Pallas kernels: 75.9 us -> 70.7 us
    pallas_call x1, Pallas kernels: 75.9 us -> 70.7 us  [local(): pl.pallas_call(functools.partial(kernel, ny, nz, scale), out_shape=jax.Sh...]
where the time goes in v3:
time: 72.4 us; the launch traced here: 72.3 us
  Pallas kernels  70.7 us (98%)
  local copies, waits for them, and re-layouts  1.57 us (2%)
    pallas_call x1, Pallas kernels, local(): pl.pallas_call(functools.partial(kernel, ny, nz, scale), out_shape=jax.Sh...  70.7 us
    unnamed x1, local copies, waits for them, and re-layouts  1.57 us

profile of v3, /device:TPU:1, one launch (start us, length us, event | category | flops | bytes accessed | tf_op | source)
XLA Modules:
  0.0 72.3 jit_solution(7295130086422150300)
XLA Ops:
  0.0 70.7 %shard_map.64 = f32[128,256]{1,0:T(8,128)} custom-call(f32[128,256]{1,0:T(8,128)} %coeffs_hbm.1, f32[2,128]{1,0:T(2,128)} %bitcast.3, f32[8,7]{1,0:T(8,128)} %w_in_hbm.1, f32[8]{0:T(128)} %b_in_hbm.1, f32[8]{0:T(128)} %w_out_hbm.1, bf16[4096,128]{1,0:T(8,128)(2,1)} %bitcast.2), custom_call_target="tpu_custom_call" | custom-call | flops 2000000000 | bytes 1500000 | tf_op jit(solution)/shard_map/pallas_call | solution.py:337
  70.7 1.6 %copy.8 = f32[128,256]{1,0:T(8,128)} copy(f32[128,256]{1,0:T(8,128)} %shard_map.64) | data formatting | bytes 262144

commit v4 on v3

--- a/solution.py
+++ b/solution.py
@@ -32,8 +32,15 @@
 
     barrier = pltpu.get_barrier_semaphore()
 
-    load = pltpu.make_async_copy(basis_hbm, raw, raw_sem)
-    load.start()
+    part = raw.shape[0] // 4
+    loads = [
+        pltpu.make_async_copy(
+            basis_hbm.at[i * part:(i + 1) * part], raw.at[i * part:(i + 1) * part], raw_sem.at[i]
+        )
+        for i in range(4)
+    ]
+    for copy in loads:
+        copy.start()
     small = [
         pltpu.make_async_copy(src, dst, small_sem.at[i])
         for i, (src, dst) in enumerate((
@@ -67,8 +74,9 @@
         & ((target & 15) == lax.shift_right_logical(source, 4)),
         1.0, 0.0,
     ).astype(bf16)
-    load.wait()
     for block in range(16):
+        if block % 4 == 0:
+            loads[block // 4].wait()
         moved = jnp.dot(
             perm, raw[block * 256:(block + 1) * 256, :], preferred_element_type=f32
         ).astype(bf16)
@@ -174,11 +182,13 @@
                     at = (2 * part + block) * 128
                     weights[at:at + 128, h * 128:(h + 1) * 128] = kept
 
-    def closure(at):
-        stack = 128 // chunk_rows
-
-        def body(i, _):
-            cells = [((i * stack + j) // 4, lax.rem(i * stack + j, 4)) for j in range(stack)]
+    inner_cells = [(1, 1), (1, 2), (2, 1), (2, 2)]
+    outer_cells = [(y, z) for y in range(4) for z in range(4) if (y, z) not in inner_cells]
+    stack = 128 // chunk_rows
+
+    def closure(at, listed):
+        for first_of in range(0, len(listed), stack):
+            cells = listed[first_of:first_of + stack]
 
             def stacked(take):
                 return jnp.concatenate([take(y, z) for y, z in cells], axis=0)
@@ -205,9 +215,6 @@
                     total = total + w_out[h] * jnp.tanh(inner)
             for j, (y, z) in enumerate(cells):
                 clos[y, z, at, :] = total[j * chunk_rows:(j + 1) * chunk_rows].astype(bf16)
-            return 0
-
-        lax.fori_loop(0, 16 // stack, body, 0, unroll=4)
 
     def project(section, offset):
         chunk, at = chunk_of(offset)
@@ -295,6 +302,8 @@
     build_weights()
     for cell in range(16):
         turned[cell * 128:(cell + 1) * 128, :] = own[cell // 4, cell % 4].T
+    for offset in order:
+        closure(chunk_of(offset)[1], inner_cells)
     sent = []
     for step, offset in enumerate(order):
         for copy in edges[step]:
@@ -302,7 +311,7 @@
         if step == min(1, chunks - 1):
             halo = basis_halo(0)
         edges_in(chunk_of(offset)[1])
-        closure(chunk_of(offset)[1])
+        closure(chunk_of(offset)[1], outer_cells)
         sent += project(0, offset)
     modal, more = reduced(0)
     halo += more
@@ -316,7 +325,7 @@
     field_y(state1)
     field_z(state1)
     for offset in order:
-        closure(chunk_of(offset)[1])
+        closure(chunk_of(offset)[1], inner_cells + outer_cells)
         sent += project(1, offset)
     modal, _ = reduced(1)
     second = scale * modal - damping * middle
@@ -367,7 +376,7 @@
             pltpu.SMEM((8, 7), f32),
             pltpu.SMEM((8,), f32),
             pltpu.SMEM((8,), f32),
-            pltpu.SemaphoreType.DMA,
+            pltpu.SemaphoreType.DMA((4,)),
             pltpu.SemaphoreType.DMA((5,)),
             pltpu.SemaphoreType.DMA((2, 2)),
             pltpu.SemaphoreType.DMA((2, 2)),

time: 72.4 us -> 71.6 us (0.989)
  Pallas kernels: 70.7 us -> 69.8 us
    pallas_call x1, Pallas kernels: 70.7 us -> 69.8 us  [local(): pl.pallas_call(functools.partial(kernel, ny, nz, scale), out_shape=jax.Sh...]
where the time goes in v4:
time: 71.6 us; the launch traced here: 71.4 us
  Pallas kernels  69.8 us (97%)
  local copies, waits for them, and re-layouts  1.57 us (2%)
    pallas_call x1, Pallas kernels, local(): pl.pallas_call(functools.partial(kernel, ny, nz, scale), out_shape=jax.Sh...  69.8 us
    unnamed x1, local copies, waits for them, and re-layouts  1.57 us

profile of v4, /device:TPU:1, one launch (start us, length us, event | category | flops | bytes accessed | tf_op | source)
XLA Modules:
  0.0 71.4 jit_solution(13175120953315523819)
XLA Ops:
  0.0 69.8 %shard_map.64 = f32[128,256]{1,0:T(8,128)} custom-call(f32[128,256]{1,0:T(8,128)} %coeffs_hbm.1, f32[2,128]{1,0:T(2,128)} %bitcast.3, f32[8,7]{1,0:T(8,128)} %w_in_hbm.1, f32[8]{0:T(128)} %b_in_hbm.1, f32[8]{0:T(128)} %w_out_hbm.1, bf16[4096,128]{1,0:T(8,128)(2,1)} %bitcast.2), custom_call_target="tpu_custom_call" | custom-call | flops 2000000000 | bytes 1500000 | tf_op jit(solution)/shard_map/pallas_call | solution.py:346
  69.8 1.6 %copy.8 = f32[128,256]{1,0:T(8,128)} copy(f32[128,256]{1,0:T(8,128)} %shard_map.64) | data formatting | bytes 262144

commit v5 on v4

--- a/solution.py
+++ b/solution.py
@@ -109,7 +109,7 @@
 
     chunks = ns // GROUP
     chunk_rows = batch // chunks
-    order = sorted(range(chunks), key=lambda o: (-min(o, chunks - o), o))
+    order = [*range(1, chunks), 0]
     my_chunk, my_place = sy // GROUP, lax.rem(sy, GROUP)
 
     def chunk_of(offset):
@@ -126,8 +126,8 @@
             for dim in range(2) for side in range(2)
         ]
 
-    def pair_field(state, first, second):
-        lhs = jnp.concatenate([state[0], state[1]], axis=1)
+    def pair_field(state, at, first, second):
+        lhs = jnp.concatenate([state[0, at, :], state[1, at, :]], axis=1)
         both = jnp.dot(lhs, jnp.concatenate([first, second], axis=1), preferred_element_type=f32)
         return both[:, :128], both[:, 128:]
 
@@ -138,27 +138,27 @@
 
     everything = slice(None)
 
-    def field_own(state, edges):
+    def field_own(state, at, edges):
         for y in range(4):
             for z in (0, 2):
-                for k, value in enumerate(pair_field(state, own[y, z], own[y, z + 1])):
-                    put(y + 1, z + k + 1, everything, value)
+                for k, value in enumerate(pair_field(state, at, own[y, z], own[y, z + 1])):
+                    put(y + 1, z + k + 1, at, value)
                     if edges and y in (0, 3):
                         edge_y[int(y == 0), z + k] = value.astype(bf16)
                     if edges and z + k in (0, 3):
                         edge_z[int(z + k == 0), y] = value.astype(bf16)
 
-    def field_y(state):
+    def field_y(state, at):
         for side, inside in ((0, sy > 0), (1, sy < ns - 1)):
             for z in (0, 2):
-                for k, value in enumerate(pair_field(state, halo_y[side, z], halo_y[side, z + 1])):
-                    put(5 * side, z + k + 1, everything, jnp.where(inside, value, 0.0))
-
-    def field_z(state):
+                for k, value in enumerate(pair_field(state, at, halo_y[side, z], halo_y[side, z + 1])):
+                    put(5 * side, z + k + 1, at, jnp.where(inside, value, 0.0))
+
+    def field_z(state, at):
         for side, inside in ((0, sz > 0), (1, sz < nz - 1)):
             for y in (0, 2):
-                for k, value in enumerate(pair_field(state, halo_z[side, y], halo_z[side, y + 1])):
-                    put(y + k + 1, 5 * side, everything, jnp.where(inside, value, 0.0))
+                for k, value in enumerate(pair_field(state, at, halo_z[side, y], halo_z[side, y + 1])):
+                    put(y + k + 1, 5 * side, at, jnp.where(inside, value, 0.0))
 
     def edges_in(at):
         for side, inside in ((0, sy > 0), (1, sy < ns - 1)):
@@ -237,6 +237,8 @@
             copies.append(copy)
         return copies
 
+    pending = []
+
     def exchange(section, phase, axis, count, src_of, dst_of):
         me = sy if axis == "sy" else sz
         copies = []
@@ -249,18 +251,20 @@
             )
             copy.start()
             copies.append(copy)
-        return copies
+        while pending:
+            pending.pop().wait_send()
+        pending.extend(copies)
+        return copies[::-1]
 
     rows_y = pl.ds(pl.multiple_of(my_y * per_y, per_y), per_y)
 
     def reduced(section):
-        for d in range(1, ns):
+        total = part_f[section, my_core, rows_y, :]
+        for d in sorted(range(1, ns), key=lambda d: -min(d, ns - d)):
             remote(
                 piece.at[section], in_y.at[section, d],
                 send_sem.at[section, 0, d], recv_sem.at[section, 0, d], {"sy": lax.rem(sy + d, ns)},
             ).wait_recv()
-        total = part_f[section, my_core, rows_y, :]
-        for d in range(1, ns):
             total = total + in_y[section, d].astype(f32)
         total = total.astype(SUM_TYPE)
         sum_y[section] = total
@@ -272,7 +276,7 @@
         between = basis_halo(1) if section == 0 else []
         in_z[section, sz] = total
         for copy in copies:
-            copy.wait()
+            copy.wait_recv()
         modal = in_z[section, 0].astype(f32)
         for z in range(1, nz):
             modal = modal + in_z[section, z].astype(f32)
@@ -287,14 +291,23 @@
             lambda d: whole.at[my_core, rows_y],
         )
         whole[my_core, rows_y, :] = block
-        for copy in copies:
-            copy.wait()
+        return copies
+
+    def gathered(section, offset):
+        chunk, _ = chunk_of(offset)
+        for i in range(int(offset == 0), GROUP):
+            source = chunk * GROUP + (lax.rem(my_place + i, GROUP) if offset == 0 else i)
+            behind = lax.rem(sy + ns - source, ns)
+            remote(
+                sum_y.at[section], piece.at[section],
+                send_sem.at[section, 2, behind], recv_sem.at[section, 2, behind], {"sy": source},
+            ).wait_recv()
 
     damping = damping_ref[pl.ds(my_core, 1), :]
     both_halves = coeffs_ref[rows_y, :]
     my_rows = jnp.where(my_core == 0, both_halves[:, :half], both_halves[:, half:])
 
-    field_own(state0, True)
+    field_own(state0, everything, True)
     edges = [edge_copies(offset) for offset in order]
     for group in edges:
         for copy in group:
@@ -304,7 +317,7 @@
         turned[cell * 128:(cell + 1) * 128, :] = own[cell // 4, cell % 4].T
     for offset in order:
         closure(chunk_of(offset)[1], inner_cells)
-    sent = []
+    pending.extend(sum(edges, []))
     for step, offset in enumerate(order):
         for copy in edges[step]:
             copy.wait_recv()
@@ -312,26 +325,32 @@
             halo = basis_halo(0)
         edges_in(chunk_of(offset)[1])
         closure(chunk_of(offset)[1], outer_cells)
-        sent += project(0, offset)
+        pending.extend(project(0, offset))
     modal, more = reduced(0)
     halo += more
     first = scale * modal - damping * my_rows
     middle = my_rows + 0.5 * first
     spread(0, middle, state1)
 
-    field_own(state1, False)
     for copy in halo:
-        copy.wait()
-    field_y(state1)
-    field_z(state1)
-    for offset in order:
+        copy.wait_recv()
+    pending.extend(halo)
+    for step, offset in enumerate(order):
+        if step < 2:
+            for chunk in order[:1] if step == 0 else order[1:]:
+                gathered(0, chunk)
+            at = chunk_of(offset)[1] if step == 0 else everything
+            field_own(state1, at, False)
+            field_y(state1, at)
+            field_z(state1, at)
         closure(chunk_of(offset)[1], inner_cells + outer_cells)
-        sent += project(1, offset)
+        pending.extend(project(1, offset))
     modal, _ = reduced(1)
     second = scale * modal - damping * middle
-    spread(1, 0.5 * (first + second), result)
-    for copy in sum(edges, sent):
-        copy.wait_send()
+    for copy in spread(1, 0.5 * (first + second), result):
+        copy.wait_recv()
+    while pending:
+        pending.pop().wait_send()
     out_ref[...] = jnp.concatenate([result[0], result[1]], axis=1).astype(f32)
 
 

time: 71.6 us -> 71.3 us (level)
  no operation moved by 1% of the time
where the time goes in v5:
time: 71.3 us; the launch traced here: 71.1 us
  Pallas kernels  69.5 us (97%)
  local copies, waits for them, and re-layouts  1.57 us (2%)
    pallas_call x1, Pallas kernels, local(): pl.pallas_call(functools.partial(kernel, ny, nz, scale), out_shape=jax.Sh...  69.5 us
    unnamed x1, local copies, waits for them, and re-layouts  1.57 us

profile of v5, /device:TPU:1, one launch (start us, length us, event | category | flops | bytes accessed | tf_op | source)
XLA Modules:
  0.0 71.1 jit_solution(7962295129561903681)
XLA Ops:
  0.0 69.5 %shard_map.64 = f32[128,256]{1,0:T(8,128)} custom-call(f32[128,256]{1,0:T(8,128)} %coeffs_hbm.1, f32[2,128]{1,0:T(2,128)} %bitcast.3, f32[8,7]{1,0:T(8,128)} %w_in_hbm.1, f32[8]{0:T(128)} %b_in_hbm.1, f32[8]{0:T(128)} %w_out_hbm.1, bf16[4096,128]{1,0:T(8,128)(2,1)} %bitcast.2), custom_call_target="tpu_custom_call" | custom-call | flops 2000000000 | bytes 1500000 | tf_op jit(solution)/shard_map/pallas_call | solution.py:365
  69.5 1.6 %copy.8 = f32[128,256]{1,0:T(8,128)} copy(f32[128,256]{1,0:T(8,128)} %shard_map.64) | data formatting | bytes 262144
